TPU v7x, 512 devices: a whole 4x8x8 slice. The times are simulated.
512 devices in a mesh: section: 32 (over x_hi, z, core), head: 16 (over y, x_lo).
Axes of the slice: x: 4 (x_hi: 2, x_lo: 2; x = x_hi * 2 + x_lo), y: 8, z: 8, core: 2. Of those that a mesh axis runs over, the one named last changes fastest.
Arguments:
- out_grad: bfloat16 [8192, 8192], P('section', 'head'), may hold values from -6 to 6
- held_query: bfloat16 [8192, 8192], P('section', 'head'), may hold values from -90 to 90
- held_output: bfloat16 [8192, 8192], P('section', 'head'), may hold values from -6 to 6
- key_cache: bfloat16 [40960, 512], P(('section', 'head')), may hold values from -4 to 4
- value_cache: bfloat16 [40960, 512], P(('section', 'head')), may hold values from -6 to 6
- segment_ids: int32 [8192], P('section'), may hold values from 0 to 511, never falling along the last dimension, each value on 1 to 64 neighbouring positions
- image_flags: int32 [8192], P('section'), may hold values 0 or 1
- cache_length: int32 [32], P('section'), may hold values from 1024 to 2048, as said below
- query_weight: bfloat16 [65536, 8192], P('section', 'head'), may hold values from -0.09375 to 0.09375
- kv_weight: bfloat16 [65536, 1024], P('section', 'head'), may hold values from -0.09375 to 0.09375
- norm_gain: bfloat16 [65536], P('section'), may hold values from 0.5 to 1.5
- layer_input: bfloat16 [8192, 4096], P(('section', 'head')), may hold values from -6 to 6
- residual_grad: bfloat16 [8192, 4096], P(('section', 'head')), may hold values from -3 to 3
Outputs:
- input_grad: bfloat16 [8192, 4096], P(('section', 'head'))
Inputs may be any that keep to these rules, and one draw needn't show every extreme that they name: `cache_length`: the two section indices 2 k and 2 k + 1 hold the same count; some section holds 2048.
All inputs are finite; a program needn't handle non-finite values. No bound on the sum of `image_flags` on one device may be relied on, other than what follows from the above.
Results may differ from a plain program's by a relative error of at most 0.0047.
Values may be sent and summed in bfloat16 or wider, within the bound.
A program may use at most 64 MiB of HBM per device.

v0:
```python
import math

import jax
import jax.numpy as jnp
from jax import lax
from jax.sharding import Mesh
from jax.sharding import PartitionSpec as P

KVH = 4
HD = 128
SL = 256
CTX = 2048
HEAD = ("head_0", "head_1")
SECTION_HEAD = ("section", "head_0", "head_1")


epsilon = 1e-06
far_negative = -1e30


def partner(value, axis, apart):
    return lax.ppermute(value, axis, [(i, i ^ 1 << apart) for i in range(lax.axis_size(axis))])


def from_everyone(value, axis):
    copies = jnp.broadcast_to(value, (lax.axis_size(axis), *value.shape))
    return lax.all_to_all(copies, axis, split_axis=0, concat_axis=0, tiled=True)


def laid_out(pieces, dim):
    pieces = jnp.moveaxis(pieces, 0, dim)
    lengths = pieces.shape
    return pieces.reshape(*lengths[:dim], lengths[dim] * lengths[dim + 1], *lengths[dim + 2 :])


def gather_directly(value, axis, dim):
    pieces = from_everyone(value, axis)
    return laid_out(pieces, dim)


def sum_by_axis(total, axes):
    for axis in axes:
        total = lax.psum_scatter(total, axis, scatter_dimension=0, tiled=True)
    return total


def contract_last(left, right):
    return lax.dot_general(
        left, right, (((1,), (1,)), ((), ())), preferred_element_type=jnp.float32
    )


def contract_first(left, right):
    return lax.dot_general(
        left, right, (((0,), (0,)), ((), ())), preferred_element_type=jnp.float32
    )


def heads_to_rows(array, local_heads):
    tokens = array.shape[0]
    return jnp.transpose(array.reshape(tokens, local_heads, HD), (1, 0, 2)).reshape(
        local_heads * tokens, HD
    )


def ordered(is_first, own_value, other_value, axis):
    return jnp.where(
        is_first,
        jnp.concatenate([own_value, other_value], axis),
        jnp.concatenate([other_value, own_value], axis),
    )


def body(
    out_grad,
    held_query,
    held_output,
    key_cache,
    value_cache,
    segment_ids,
    image_flags,
    cache_length,
    query_weight,
    kv_weight,
    norm_gain,
    layer_input,
    residual_grad,
):
    head_count = lax.axis_size(HEAD)
    section_count = lax.axis_size("section")
    section_bits = section_count.bit_length() - 1
    parity = lax.axis_index("section") % 2
    is_first = parity == 0
    local_heads = out_grad.shape[1] // HD
    group_index = lax.axis_index(HEAD) // (head_count // KVH)
    factor = 1.0 / math.sqrt(HD)
    stash_pair = jnp.stack([held_query, held_output])
    for bit_level in range(1, section_bits):
        stash_pair = partner(stash_pair, "section", bit_level)
    other_segments, other_flags = partner((segment_ids, image_flags), "section", 0)
    segments_all = ordered(is_first, segment_ids, other_segments, 0)
    flags_all = ordered(is_first, image_flags, other_flags, 0)
    pair_rows = jnp.stack([key_cache, value_cache])
    gathered = lax.all_gather(pair_rows, HEAD, axis=1, tiled=True)
    own_half = lax.dynamic_slice_in_dim(gathered, group_index * HD, HD, 2)
    other_half, other_gain = partner((own_half, norm_gain), "section", 0)
    both_halves = ordered(is_first, own_half, other_half, 1)
    key_rows = both_halves[0]
    value_rows = both_halves[1]
    gain_full = ordered(is_first, norm_gain, other_gain, 0)
    query_rows = heads_to_rows(stash_pair[0], local_heads)
    output_rows = heads_to_rows(stash_pair[1], local_heads)
    grad_rows = heads_to_rows(out_grad, local_heads)
    row_delta = jnp.sum(grad_rows.astype(jnp.float32) * output_rows.astype(jnp.float32), axis=1)
    token_here = parity * SL + jnp.tile(jnp.arange(SL, dtype=jnp.int32), local_heads)
    row_segments = jnp.tile(segment_ids, local_heads)
    row_flags = jnp.tile(image_flags, local_heads)
    key_block = math.gcd(CTX, 512)
    cache_blocks = CTX // key_block
    length = cache_length[0]

    def cache_scores(block_index):
        block_keys = lax.dynamic_slice_in_dim(key_rows, block_index * key_block, key_block, 0)
        block_values = lax.dynamic_slice_in_dim(value_rows, block_index * key_block, key_block, 0)
        scores = contract_last(query_rows, block_keys) * factor
        valid = block_index * key_block + jnp.arange(key_block, dtype=jnp.int32) < length
        return (jnp.where(valid[None, :], scores, far_negative), block_keys, block_values)

    slice_keys = key_rows[CTX:]
    slice_values = value_rows[CTX:]
    same_segment = row_segments[:, None] == segments_all[None, :]
    both_image = (row_flags[:, None] == 1) & (flags_all[None, :] == 1)
    slice_ok = same_segment & (
        (jnp.arange(2 * SL, dtype=jnp.int32)[None, :] <= token_here[:, None]) | both_image
    )
    slice_scores = jnp.where(slice_ok, contract_last(query_rows, slice_keys) * factor, far_negative)
    start_max = jnp.max(slice_scores, axis=1)
    start_sum = jnp.sum(jnp.exp(slice_scores - start_max[:, None]), axis=1)

    def first_pass(running, block_index):
        running_max, running_sum = running
        scores, unused_keys, unused_values = cache_scores(block_index)
        new_max = jnp.maximum(running_max, jnp.max(scores, axis=1))
        running_sum = running_sum * jnp.exp(running_max - new_max) + jnp.sum(
            jnp.exp(scores - new_max[:, None]), axis=1
        )
        return ((new_max, running_sum), None)

    (final_max, final_sum), unused_out = lax.scan(
        first_pass, (start_max, start_sum), jnp.arange(cache_blocks)
    )
    log_total = final_max + jnp.log(final_sum)

    def gradient_terms(scores, block_keys, block_values):
        attn_probs = jnp.exp(scores - log_total[:, None])
        prob_grad = contract_last(grad_rows, block_values)
        score_grad = (attn_probs * (prob_grad - row_delta[:, None]) * factor).astype(jnp.bfloat16)
        return (
            attn_probs,
            score_grad,
            jnp.dot(score_grad, block_keys, preferred_element_type=jnp.float32),
        )

    slice_probs, slice_grad, slice_term = gradient_terms(slice_scores, slice_keys, slice_values)

    def second_pass(running, block_index):
        scores, block_keys, block_values = cache_scores(block_index)
        unused_probs, unused_grad, block_term = gradient_terms(scores, block_keys, block_values)
        return (running + block_term, None)

    query_total, unused_out = lax.scan(second_pass, slice_term, jnp.arange(cache_blocks))
    query_grad = jnp.transpose(
        query_total.astype(jnp.bfloat16).reshape(local_heads, SL, HD), (1, 0, 2)
    ).reshape(SL, local_heads * HD)
    key_grad = contract_first(slice_grad, query_rows)
    value_grad = contract_first(slice_probs.astype(jnp.bfloat16), grad_rows)
    kv_width = 2 * KVH * HD
    column_width = kv_width // head_count
    sharers = head_count // KVH
    member = lax.axis_index(HEAD) % sharers
    piece_width = HD // sharers
    current = jnp.stack([key_grad, value_grad], 1).reshape(2 * SL, 2, sharers, piece_width)
    level_count = sharers.bit_length() - 1
    for bit_level in reversed(range(level_count)):
        half = current.shape[2] // 2
        lower_part = current[:, :, :half]
        upper_part = current[:, :, half:]
        high_side = member // (1 << bit_level) % 2 == 1
        kept = jnp.where(high_side, upper_part, lower_part)
        sent = jnp.where(high_side, lower_part, upper_part)
        current = kept + partner(sent, HEAD, bit_level)
    kv_columns = current.reshape(2 * SL, 2 * piece_width)
    kv_total = kv_columns + partner(kv_columns, "section", 0)
    kv_part = kv_total.astype(jnp.bfloat16)
    collected_kv = gather_directly(kv_part, HEAD, 1)
    arranged = jnp.transpose(
        collected_kv.reshape(2 * SL, KVH, sharers, 2, piece_width), (0, 3, 1, 2, 4)
    ).reshape(2 * SL, kv_width)
    kv_rounded = lax.dynamic_slice_in_dim(
        arranged, lax.axis_index(HEAD) * column_width, column_width, 1
    )
    other_query_w, other_kv_w = partner((query_weight, kv_weight), "section", 0)
    query_full = ordered(is_first, query_weight, other_query_w, 0)
    kv_full = ordered(is_first, kv_weight, other_kv_w, 0)
    own_kv = lax.dynamic_slice_in_dim(kv_rounded, parity * SL, SL, 0)
    normed_grad = sum_by_axis(
        contract_last(query_grad, query_full) + contract_last(own_kv, kv_full), HEAD
    )
    values_in = layer_input.astype(jnp.float32)
    inverse = lax.rsqrt(jnp.mean(values_in * values_in, axis=1, keepdims=True) + epsilon)
    weighted = gain_full.astype(jnp.float32)[None, :] * normed_grad
    result = (
        residual_grad.astype(jnp.float32)
        + inverse * weighted
        - values_in * inverse**3 * jnp.mean(weighted * values_in, axis=1, keepdims=True)
    )
    return result.astype(jnp.bfloat16)


def solution(mesh):
    finer = Mesh(mesh.devices.reshape(mesh.shape["section"], 8, 2), ("section", "head_0", "head_1"))
    in_specs = (
        P("section", HEAD),
        P("section", HEAD),
        P("section", HEAD),
        P(SECTION_HEAD, None),
        P(SECTION_HEAD, None),
        P("section"),
        P("section"),
        P("section"),
        P("section", HEAD),
        P("section", HEAD),
        P("section"),
        P(SECTION_HEAD, None),
        P(SECTION_HEAD, None),
    )
    out_specs = P(SECTION_HEAD, None)
    return jax.shard_map(body, mesh=finer, in_specs=in_specs, out_specs=out_specs, check_vma=False)
```

profile of v0, /device:TPU:1, one launch (start us, length us, event | category | flops | bytes accessed | tf_op | source)
XLA Modules:
  0.0 277.3 jit_solution(12912714254418523092)
XLA Ops:
  6.5 1.7 pad_maximum_fusion.2
  8.2 1.1 pad_maximum_fusion
  9.3 4.8 %collective-permute-start.3 = (bf16[2,256,512]{2,1,0:T(8,128)(2,1)S(1)}, bf16[2,256,512]{2,1,0:T(8,128)(2,1)S(1)}, u32[]{:S(2)}, u32[]{:S(2)}) collective-permute-start(bf16[2,256,512]{2,1,0:T(8,128)(2,1)S(1)} %pad_maximum_fusion), channel_id=1, source_target_pairs={{0,32},{16,48},{32,0},{48,16},{64,96},{80,112},{96,64},{112,80},{1... | collective-permute-start | bytes 1572872 | tf_op jit(solution)/shard_map/ppermute | solution.py:22
  14.2 7.5 %collective-permute-done.3 = bf16[2,256,512]{2,1,0:T(8,128)(2,1)S(1)} collective-permute-done((bf16[2,256,512]{2,1,0:T(8,128)(2,1)S(1)}, bf16[2,256,512]{2,1,0:T(8,128)(2,1)S(1)}, u32[]{:S(2)}, u32[]{:S(2)}) %collective-permute-start.3) | collective-permute-done | bytes 524320 | tf_op jit(solution)/shard_map/ppermute | solution.py:22
  21.7 9.9 %collective-permute-start.4 = (bf16[2,256,512]{2,1,0:T(8,128)(2,1)S(1)}, bf16[2,256,512]{2,1,0:T(8,128)(2,1)S(1)}, u32[]{:S(2)}, u32[]{:S(2)}) collective-permute-start(bf16[2,256,512]{2,1,0:T(8,128)(2,1)S(1)} %collective-permute-done.3), channel_id=1, source_target_pairs={{0,64},{16,80},{32,96},{48,112},{64,0},{80,16},{96,32},{112,48},{1... | collective-permute-start | bytes 1572872 | tf_op jit(solution)/shard_map/ppermute | solution.py:22
  31.6 22.7 %collective-permute-done.4 = bf16[2,256,512]{2,1,0:T(8,128)(2,1)S(1)} collective-permute-done((bf16[2,256,512]{2,1,0:T(8,128)(2,1)S(1)}, bf16[2,256,512]{2,1,0:T(8,128)(2,1)S(1)}, u32[]{:S(2)}, u32[]{:S(2)}) %collective-permute-start.4) | collective-permute-done | bytes 524320 | tf_op jit(solution)/shard_map/ppermute | solution.py:22
  54.3 8.1 %collective-permute-start.5 = (bf16[2,256,512]{2,1,0:T(8,128)(2,1)S(1)}, bf16[2,256,512]{2,1,0:T(8,128)(2,1)S(1)}, u32[]{:S(2)}, u32[]{:S(2)}) collective-permute-start(bf16[2,256,512]{2,1,0:T(8,128)(2,1)S(1)} %collective-permute-done.4), channel_id=1, source_target_pairs={{0,128},{16,144},{32,160},{48,176},{64,192},{80,208},{96,224},{112... | collective-permute-start | bytes 1572872 | tf_op jit(solution)/shard_map/ppermute | solution.py:22
  62.5 3.6 %collective-permute-start.1 = (s32[256]{0:T(256)}, s32[256]{0:T(256)S(1)}, u32[]{:S(2)}, u32[]{:S(2)}) collective-permute-start(s32[256]{0:T(256)} %param.22), channel_id=1, source_target_pairs={{0,16},{16,0},{32,48},{48,32},{64,80},{80,64},{96,112},{112,96},{1... | collective-permute-start | bytes 3080 | tf_op jit(solution)/shard_map/ppermute | solution.py:22
  66.0 1.9 collective-permute-start.2
  68.0 0.7 broadcast_compare_fusion
  68.7 0.7 broadcast_bitcast_fusion
  69.4 15.3 %collective-permute-done.5 = bf16[2,256,512]{2,1,0:T(8,128)(2,1)S(1)} collective-permute-done((bf16[2,256,512]{2,1,0:T(8,128)(2,1)S(1)}, bf16[2,256,512]{2,1,0:T(8,128)(2,1)S(1)}, u32[]{:S(2)}, u32[]{:S(2)}) %collective-permute-start.5) | collective-permute-done | bytes 524320 | tf_op jit(solution)/shard_map/ppermute | solution.py:22
  84.6 4.5 %collective-permute-start.6 = (bf16[2,256,512]{2,1,0:T(8,128)(2,1)S(1)}, bf16[2,256,512]{2,1,0:T(8,128)(2,1)S(1)}, u32[]{:S(2)}, u32[]{:S(2)}) collective-permute-start(bf16[2,256,512]{2,1,0:T(8,128)(2,1)S(1)} %collective-permute-done.5), channel_id=1, source_target_pairs={{0,256},{16,272},{32,288},{48,304},{64,320},{80,336},{96,352},{112... | collective-permute-start | bytes 1572872 | tf_op jit(solution)/shard_map/ppermute | solution.py:22
  89.1 1.1 constant_dynamic-slice_fusion
  90.3 7.3 %collective-permute-start.7 = (bf16[2,1280,128]{2,1,0:T(8,128)(2,1)S(1)}, bf16[2,1280,128]{2,1,0:T(8,128)(2,1)S(1)}, u32[]{:S(2)}, u32[]{:S(2)}) collective-permute-start(bf16[2,1280,128]{2,1,0:T(8,128)(2,1)S(1)} %constant_dynamic-slice_fusion), channel_id=1, source_target_pairs={{0,16},{16,0},{32,48},{48,32},{64,80},{80,64},{96,112},{112,96},{1... | collective-permute-start | bytes 1966088 | tf_op jit(solution)/shard_map/ppermute | solution.py:22
  98.1 4.3 %collective-permute-done.6 = bf16[2,256,512]{2,1,0:T(8,128)(2,1)S(1)} collective-permute-done((bf16[2,256,512]{2,1,0:T(8,128)(2,1)S(1)}, bf16[2,256,512]{2,1,0:T(8,128)(2,1)S(1)}, u32[]{:S(2)}, u32[]{:S(2)}) %collective-permute-start.6) | collective-permute-done | bytes 524320 | tf_op jit(solution)/shard_map/ppermute | solution.py:22
  103.3 0.9 copy.35
  104.5 1.0 slice_bitcast_fusion
  105.5 0.9 fusion.56
  106.8 11.9 %while.22 = (s32[]{:T(128)}, f32[1024]{0:T(1024)S(1)}, f32[1024]{0:T(1024)S(1)}, s32[4]{0:T(128)S(1)}, s32[]{:T(128)}, /*index=5*/bf16[2560,128]{1,0:T(8,128)(2,...) while((s32[]{:T(128)}, f32[1024]{0:T(1024)S(1)}, ...), condition=%wide.region_6.7_spmd, body=%wide.region_3.6_spmd.sunk | while | flops 137890816 | bytes 4642491 | solution.py:149
  106.8 0.7 dynamic_slice.46
  119.3 1.5 fusion.28
  120.8 1.0 copy-done.1
  122.3 2.8 %collective-permute-start.9 = (f32[512,2,2,32]{0,3,2,1:T(8,128)S(1)}, f32[512,2,2,32]{0,3,2,1:T(8,128)S(1)}, u32[]{:S(2)}, u32[]{:S(2)}) collective-permute-start(f32[512,2,2,32]{0,3,2,1:T(8,128)S(1)} %broadcast_select_fusion), channel_id=1, source_target_pairs={{0,2},{1,3},{2,0},{3,1},{4,6},{5,7},{6,4},{7,5},{8,10},{9,11},{10,... | collective-permute-start | bytes 786440 | tf_op jit(solution)/shard_map/ppermute | solution.py:22
  125.1 5.3 %collective-permute-done.9 = f32[512,2,2,32]{0,3,2,1:T(8,128)S(1)} collective-permute-done((f32[512,2,2,32]{0,3,2,1:T(8,128)S(1)}, f32[512,2,2,32]{0,3,2,1:T(8,128)S(1)}, u32[]{:S(2)}, u32[]{:S(2)}) %collective-permute-start.9) | collective-permute-done | bytes 262176 | tf_op jit(solution)/shard_map/ppermute | solution.py:22
  130.5 2.8 %collective-permute-start.10 = (f32[512,2,1,32]{0,3,2,1:T(8,128)S(1)}, f32[512,2,1,32]{0,3,2,1:T(8,128)S(1)}, u32[]{:S(2)}, u32[]{:S(2)}) collective-permute-start(f32[512,2,1,32]{0,3,2,1:T(8,128)S(1)} %slice_select_fusion), channel_id=1, source_target_pairs={{0,1},{1,0},{2,3},{3,2},{4,5},{5,4},{6,7},{7,6},{8,9},{9,8},{10,11... | collective-permute-start | bytes 393224 | tf_op jit(solution)/shard_map/ppermute | solution.py:22
  133.3 4.8 %collective-permute-start.12 = (bf16[2048,64]{0,1:T(8,128)(2,1)}, bf16[2048,64]{0,1:T(8,128)(2,1)}, u32[]{:S(2)}, u32[]{:S(2)}) collective-permute-start(bf16[2048,64]{0,1:T(8,128)(2,1)} %param.26), channel_id=1, source_target_pairs={{0,16},{16,0},{32,48},{48,32},{64,80},{80,64},{96,112},{112,96},{1... | collective-permute-start | bytes 786440 | tf_op jit(solution)/shard_map/ppermute | solution.py:22
  138.1 1.9 collective-permute-start.8
  140.1 0.8 copy.33
  140.9 2.4 collective-permute-start.11
  143.4 1.4 fusion.50
  144.8 1.1 broadcast_in_dim.43
  145.9 5.5 %all-to-all-start = ((bf16[16,512,64]{1,2,0:T(8,128)(2,1)}), bf16[16,512,64]{1,2,0:T(8,128)(2,1)}, u32[]{:S(2)}, u32[]{:S(2)}) async-start(bf16[16,512,64]{1,2,0:T(8,128)(2,1)} %broadcast_in_dim.43), calls=%async_computation | async-start | bytes 2097152 | tf_op jit(solution)/shard_map/all_to_all | solution.py:27
  151.6 18.6 %while.23 = (s32[]{:T(128)}, f32[1024,128]{1,0:T(8,128)S(1)}, s32[4]{0:T(128)S(1)}, s32[]{:T(128)}, bf16[2560,128]{1,0:T(8,128)(2,1)S(1)}, /*index=5*/bf16[1024,...) while((s32[]{:T(128)}, f32[1024,128]{1,0:T(8,128)S(1)}, ...), condition=%wide.region_9.10_spmd, body=%wide.region_8.9_spmd.sunk | while | flops 406455296 | bytes 6170835 | solution.py:171
  154.0 2.3 fusion.83
  158.6 2.3 fusion.83
  163.3 2.3 fusion.83
  167.9 2.3 fusion.83
  170.4 7.3 %all-to-all-done = bf16[16,512,64]{1,2,0:T(8,128)(2,1)} async-done(((bf16[16,512,64]{1,2,0:T(8,128)(2,1)}), bf16[16,512,64]{1,2,0:T(8,128)(2,1)}, u32[]{:S(2)}, u32[]{:S(2)}) %all-to-all-start) | async-done | bytes 1048608 | tf_op jit(solution)/shard_map/all_to_all | solution.py:27
  177.7 1.3 copy.38
  179.0 2.1 fusion.36
  181.2 5.6 %convolution_add_fusion = f32[256,4096]{1,0:T(8,128)} fusion(f32[256,4096]{1,0:T(8,128)S(1)} %fusion.36, bf16[256,512]{0,1:T(8,128)(2,1)S(1)} %bitcast.106, bf16[2048,512]{1,0:T(8,128)(2,1)} %collective-permute-done.8, bf16[2048,512]{1,0:T(8,128)(2,1)S(1)} %copy-done.10, pred[]{:T(512)S(6)} %eq.55), kind=kOutput, calls=%fused_computation.25 | convolution fusion | flops 1093664768 | bytes 12845057 | tf_op jit(solution)/shard_map/dot_general | solution.py:48
  186.8 56.7 %reduce-scatter.3.cloned.1.call-done = f32[32,4096]{1,0:T(8,128)} async-done(((f32[256,4096]{1,0:T(8,128)}), f32[32,4096]{1,0:T(8,128)}) %reduce-scatter.3.cloned.1.call-update) | async-done | bytes 524304 | tf_op jit(solution)/shard_map/reduce_scatter | solution.py:43
  243.6 2.5 collective-permute-start
  246.1 0.8 collective-permute-done
  246.9 20.9 %reduce-scatter.5.cloned.1.call-done = f32[16,4096]{1,0:T(8,128)} async-done(((f32[32,4096]{1,0:T(8,128)}), f32[16,4096]{1,0:T(8,128)}) %reduce-scatter.5.cloned.1.call-update) | async-done | bytes 262160 | tf_op jit(solution)/shard_map/reduce_scatter | solution.py:43
  267.9 1.1 fusion.44
  269.0 1.7 fusion.47
  (107 shorter events, 18.8 us)
Async XLA Ops:
  6.5 91.1 %copy-start.4 = (bf16[256,512]{1,0:T(8,128)(2,1)S(1)}, bf16[256,512]{1,0:T(8,128)(2,1)}, u32[]{:S(2)}) copy-start(bf16[256,512]{1,0:T(8,128)(2,1)} %param.17) | copy-start | bytes 786436
  6.5 82.6 %all-gather.2.cloned.1.call-start = ((), (), s32[]{:S(2)}) async-start(), calls=%async_computation.3 | async-start | bytes 2785280 | tf_op jit(solution)/shard_map/all_gather | solution.py:104
  8.2 89.8 %copy-start.9 = (s32[256]{0:T(256)S(1)}, s32[256]{0:T(256)}, u32[]{:S(2)}) copy-start(s32[256]{0:T(256)} %param.23) | copy-start | bytes 3076
  8.2 89.8 %copy-start.8 = (s32[256]{0:T(256)S(1)}, s32[256]{0:T(256)}, u32[]{:S(2)}) copy-start(s32[256]{0:T(256)} %param.22) | copy-start | bytes 3076
  9.3 12.4 %collective-permute-start.3 = (bf16[2,256,512]{2,1,0:T(8,128)(2,1)S(1)}, bf16[2,256,512]{2,1,0:T(8,128)(2,1)S(1)}, u32[]{:S(2)}, u32[]{:S(2)}) collective-permute-start(bf16[2,256,512]{2,1,0:T(8,128)(2,1)S(1)} %pad_maximum_fusion), channel_id=1, source_target_pairs={{0,32},{16,48},{32,0},{48,16},{64,96},{80,112},{96,64},{112,80},{1... | collective-permute-start | bytes 1572872 | tf_op jit(solution)/shard_map/ppermute | solution.py:22
  21.7 32.6 %collective-permute-start.4 = (bf16[2,256,512]{2,1,0:T(8,128)(2,1)S(1)}, bf16[2,256,512]{2,1,0:T(8,128)(2,1)S(1)}, u32[]{:S(2)}, u32[]{:S(2)}) collective-permute-start(bf16[2,256,512]{2,1,0:T(8,128)(2,1)S(1)} %collective-permute-done.3), channel_id=1, source_target_pairs={{0,64},{16,80},{32,96},{48,112},{64,0},{80,16},{96,32},{112,48},{1... | collective-permute-start | bytes 1572872 | tf_op jit(solution)/shard_map/ppermute | solution.py:22
  54.3 30.3 %collective-permute-start.5 = (bf16[2,256,512]{2,1,0:T(8,128)(2,1)S(1)}, bf16[2,256,512]{2,1,0:T(8,128)(2,1)S(1)}, u32[]{:S(2)}, u32[]{:S(2)}) collective-permute-start(bf16[2,256,512]{2,1,0:T(8,128)(2,1)S(1)} %collective-permute-done.4), channel_id=1, source_target_pairs={{0,128},{16,144},{32,160},{48,176},{64,192},{80,208},{96,224},{112... | collective-permute-start | bytes 1572872 | tf_op jit(solution)/shard_map/ppermute | solution.py:22
  62.5 35.6 %collective-permute-start.1 = (s32[256]{0:T(256)}, s32[256]{0:T(256)S(1)}, u32[]{:S(2)}, u32[]{:S(2)}) collective-permute-start(s32[256]{0:T(256)} %param.22), channel_id=1, source_target_pairs={{0,16},{16,0},{32,48},{48,32},{64,80},{80,64},{96,112},{112,96},{1... | collective-permute-start | bytes 3080 | tf_op jit(solution)/shard_map/ppermute | solution.py:22
  66.0 32.0 %collective-permute-start.2 = (s32[256]{0:T(256)}, s32[256]{0:T(256)S(1)}, u32[]{:S(2)}, u32[]{:S(2)}) collective-permute-start(s32[256]{0:T(256)} %param.23), channel_id=1, source_target_pairs={{0,16},{16,0},{32,48},{48,32},{64,80},{80,64},{96,112},{112,96},{1... | collective-permute-start | bytes 3080 | tf_op jit(solution)/shard_map/ppermute | solution.py:22
  84.6 17.8 %collective-permute-start.6 = (bf16[2,256,512]{2,1,0:T(8,128)(2,1)S(1)}, bf16[2,256,512]{2,1,0:T(8,128)(2,1)S(1)}, u32[]{:S(2)}, u32[]{:S(2)}) collective-permute-start(bf16[2,256,512]{2,1,0:T(8,128)(2,1)S(1)} %collective-permute-done.5), channel_id=1, source_target_pairs={{0,256},{16,272},{32,288},{48,304},{64,320},{80,336},{96,352},{112... | collective-permute-start | bytes 1572872 | tf_op jit(solution)/shard_map/ppermute | solution.py:22
  90.3 13.9 %collective-permute-start.7 = (bf16[2,1280,128]{2,1,0:T(8,128)(2,1)S(1)}, bf16[2,1280,128]{2,1,0:T(8,128)(2,1)S(1)}, u32[]{:S(2)}, u32[]{:S(2)}) collective-permute-start(bf16[2,1280,128]{2,1,0:T(8,128)(2,1)S(1)} %constant_dynamic-slice_fusion), channel_id=1, source_target_pairs={{0,16},{16,0},{32,48},{48,32},{64,80},{80,64},{96,112},{112,96},{1... | collective-permute-start | bytes 1966088 | tf_op jit(solution)/shard_map/ppermute | solution.py:22
  104.5 2.0 copy-start
  119.3 2.5 copy-start.5
  120.8 1.0 copy-start.1
  122.3 21.1 %copy-start.2 = (bf16[1024,512]{0,1:T(8,128)(2,1)S(1)}, bf16[1024,512]{0,1:T(8,128)(2,1)}, u32[]{:S(2)}) copy-start(bf16[1024,512]{0,1:T(8,128)(2,1)} %copy-done.1) | copy-start | bytes 3145732
  122.3 8.1 %collective-permute-start.9 = (f32[512,2,2,32]{0,3,2,1:T(8,128)S(1)}, f32[512,2,2,32]{0,3,2,1:T(8,128)S(1)}, u32[]{:S(2)}, u32[]{:S(2)}) collective-permute-start(f32[512,2,2,32]{0,3,2,1:T(8,128)S(1)} %broadcast_select_fusion), channel_id=1, source_target_pairs={{0,2},{1,3},{2,0},{3,1},{4,6},{5,7},{6,4},{7,5},{8,10},{9,11},{10,... | collective-permute-start | bytes 786440 | tf_op jit(solution)/shard_map/ppermute | solution.py:22
  130.5 10.4 %collective-permute-start.10 = (f32[512,2,1,32]{0,3,2,1:T(8,128)S(1)}, f32[512,2,1,32]{0,3,2,1:T(8,128)S(1)}, u32[]{:S(2)}, u32[]{:S(2)}) collective-permute-start(f32[512,2,1,32]{0,3,2,1:T(8,128)S(1)} %slice_select_fusion), channel_id=1, source_target_pairs={{0,1},{1,0},{2,3},{3,2},{4,5},{5,4},{6,7},{7,6},{8,9},{9,8},{10,11... | collective-permute-start | bytes 393224 | tf_op jit(solution)/shard_map/ppermute | solution.py:22
  133.3 45.7 %collective-permute-start.12 = (bf16[2048,64]{0,1:T(8,128)(2,1)}, bf16[2048,64]{0,1:T(8,128)(2,1)}, u32[]{:S(2)}, u32[]{:S(2)}) collective-permute-start(bf16[2048,64]{0,1:T(8,128)(2,1)} %param.26), channel_id=1, source_target_pairs={{0,16},{16,0},{32,48},{48,32},{64,80},{80,64},{96,112},{112,96},{1... | collective-permute-start | bytes 786440 | tf_op jit(solution)/shard_map/ppermute | solution.py:22
  138.1 43.0 %collective-permute-start.8 = (bf16[2048,512]{1,0:T(8,128)(2,1)}, bf16[2048,512]{1,0:T(8,128)(2,1)}, u32[]{:S(2)}, u32[]{:S(2)}) collective-permute-start(bf16[2048,512]{1,0:T(8,128)(2,1)} %param.25), channel_id=1, source_target_pairs={{0,16},{16,0},{32,48},{48,32},{64,80},{80,64},{96,112},{112,96},{1... | collective-permute-start | bytes 6291464 | tf_op jit(solution)/shard_map/ppermute | solution.py:22
  140.9 3.8 %collective-permute-start.11 = (f32[512,64]{0,1:T(8,128)S(1)}, f32[512,64]{0,1:T(8,128)S(1)}, u32[]{:S(2)}, u32[]{:S(2)}) collective-permute-start(f32[512,64]{0,1:T(8,128)S(1)} %bitcast.104), channel_id=1, source_target_pairs={{0,16},{16,0},{32,48},{48,32},{64,80},{80,64},{96,112},{112,96},{1... | collective-permute-start | bytes 393224 | tf_op jit(solution)/shard_map/ppermute | solution.py:22
  145.9 31.8 %all-to-all-start = ((bf16[16,512,64]{1,2,0:T(8,128)(2,1)}), bf16[16,512,64]{1,2,0:T(8,128)(2,1)}, u32[]{:S(2)}, u32[]{:S(2)}) async-start(bf16[16,512,64]{1,2,0:T(8,128)(2,1)} %broadcast_in_dim.43), calls=%async_computation | async-start | bytes 2097152 | tf_op jit(solution)/shard_map/all_to_all | solution.py:27
  151.4 92.2 %reduce-scatter.3.cloned.1.call-start = ((), (), s32[]{:S(2)}) async-start(), calls=%async_computation.4 | async-start | bytes 4718592 | tf_op jit(solution)/shard_map/reduce_scatter | solution.py:43
  179.0 2.2 copy-start.10
  186.8 56.8 %copy-start.7 = (bf16[2048]{0:T(1024)(128)(2,1)S(1)}, bf16[2048]{0:T(1024)(128)(2,1)}, u32[]{:S(2)}) copy-start(bf16[2048]{0:T(1024)(128)(2,1)} %param.27) | copy-start | bytes 12292
  186.8 81.1 %copy-start.3 = (bf16[16,4096]{1,0:T(8,128)(2,1)S(1)}, bf16[16,4096]{1,0:T(8,128)(2,1)}, u32[]{:S(2)}) copy-start(bf16[16,4096]{1,0:T(8,128)(2,1)} %param.28) | copy-start | bytes 393220
  186.8 82.2 %copy-start.6 = (bf16[16,4096]{1,0:T(8,128)(2,1)S(1)}, bf16[16,4096]{1,0:T(8,128)(2,1)}, u32[]{:S(2)}) copy-start(bf16[16,4096]{1,0:T(8,128)(2,1)} %param.29) | copy-start | bytes 393220
  186.8 81.0 %reduce-scatter.5.cloned.1.call-start = ((), (), s32[]{:S(2)}) async-start(), calls=%async_computation.5 | async-start | bytes 786432 | tf_op jit(solution)/shard_map/reduce_scatter | solution.py:43
  243.6 3.3 %collective-permute-start = (bf16[2048]{0:T(1024)(128)(2,1)S(1)}, bf16[2048]{0:T(1024)(128)(2,1)S(1)}, u32[]{:S(2)}, u32[]{:S(2)}) collective-permute-start(bf16[2048]{0:T(1024)(128)(2,1)S(1)} %copy-done.7), channel_id=1, source_target_pairs={{0,16},{16,0},{32,48},{48,32},{64,80},{80,64},{96,112},{112,96},{1... | collective-permute-start | bytes 12296 | tf_op jit(solution)/shard_map/ppermute | solution.py:22
Sparse Core Ops, SparseCore 0:
  9.4 76.6 all-gather.1
  186.9 56.5 reduce-scatter.2
  246.3 21.4 reduce-scatter.4
where the time goes:
time: 278 us; the launch traced here: 277 us
  waiting for transfers between devices  141 us (51%)
  starting transfers between devices  63.1 us (23%)
  matrix products  25.3 us (9%)
  other arithmetic  14.7 us (5%)
  local copies, waits for them, and re-layouts  14 us (5%)
  between operations  13.7 us (5%)
  loops' own time  5.49 us (2%)
    reduce_scatter x2, waiting for transfers between devices, sum_by_axis(): total = lax.psum_scatter(total, axis, scatter_dimension=0, tiled=True)  77.6 us
    ppermute x13, starting transfers between devices, partner(): lax.ppermute(value, axis, [(i, i ^ 1 << apart) for i in range(lax.axis_si...  57.3 us
    ppermute x13, waiting for transfers between devices, partner(): lax.ppermute(value, axis, [(i, i ^ 1 << apart) for i in range(lax.axis_si...  56 us
    dot_general x12, matrix products, contract_last(): lax.dot_general(left, right, (((1,), (1,)), ((), ())), preferred_element_...  13.7 us
    dot_general x5, matrix products, gradient_terms(): jnp.dot(score_grad, block_keys, preferred_element_type=jnp.float32)  10.5 us
    all_to_all x1, waiting for transfers between devices, from_everyone(): return lax.all_to_all(copies, axis, split_axis=0, concat_axis=0, tiled=True)  7.3 us
  transfers between devices with their start and end apart: 17, of which 9 were waited for; matrix products, arithmetic and copies ran while one was open for 10% of the time, Pallas kernels for 0%

commit v1 on v0

v1 whole, which is shorter than its diff:
```python
import math

import jax
import jax.numpy as jnp
from jax import lax
from jax.experimental import pallas as pl
from jax.experimental.pallas import tpu as pltpu
from jax.sharding import PartitionSpec as P

MESH = pl.DeviceIdType.MESH
BF16, F32 = jnp.bfloat16, jnp.float32

KVH = 4
HD = 128
SL = 256
CTX = 2048
D = 4096
LOCAL = 4
HEADS = 16
RING = 8
GROUP = HEADS // KVH
OWN = (CTX + 2 * SL) // 2 // HEADS
HALF = (CTX + 2 * SL) // 2
WINDOW = 384
CHUNK = 512
BLOCK = 512
BLOCKS = D // BLOCK

epsilon = 1e-06
far_negative = -1e30
factor = 1.0 / math.sqrt(HD)
factor2 = factor / math.log(2.0)


def x_first(block):
    return block % 2 == 0


def dot_nt(left, right):
    return lax.dot_general(left, right, (((1,), (1,)), ((), ())), preferred_element_type=F32)


def dot_tn(left, right):
    return lax.dot_general(left, right, (((0,), (0,)), ((), ())), preferred_element_type=F32)


def kernel(
    out_grad,
    held_query,
    held_output,
    key_cache,
    value_cache,
    code_row,
    length,
    query_weight,
    kv_weight,
    gain,
    layer_input,
    residual,
    result,
    queries,
    outputs,
    grads,
    keys,
    values,
    q_rows,
    kv_rows,
    codes,
    gains,
    scores,
    bias,
    query_grad,
    kv_acc,
    kv_other,
    kv_out,
    kv_in,
    acc,
    x_out,
    x_in,
    ring_out,
    ring_in,
    normed,
    own_sem,
    mirror_send,
    mirror_recv,
    gather_send,
    gather_recv,
    pair_send,
    pair_recv,
    share_send,
    share_recv,
    ring_send,
    ring_recv,
    x_send,
    x_recv,
):
    section = lax.axis_index("section")
    head = lax.axis_index("head")
    core = section % 2
    ring_at = head // 2
    side = head % 2
    mirror = (30 - section + 2 * core, head)
    pair = (section + 1 - 2 * core, head)
    across = (section, head + 1 - 2 * side)
    along = ((section, (head + 2) % HEADS), (section, (head + HEADS - 2) % HEADS))

    barrier = pltpu.get_barrier_semaphore()
    peers = [mirror, pair] + [(section, (head + i) % HEADS) for i in range(1, HEADS)]
    for peer in peers:
        pl.semaphore_signal(barrier, inc=1, device_id=peer, device_id_type=MESH)

    def mine(i, source, target):
        return pltpu.make_async_copy(source, target, own_sem.at[i])

    def remote(source, target, send, recv, device):
        return pltpu.make_async_remote_copy(
            src_ref=source, dst_ref=target, send_sem=send, recv_sem=recv,
            device_id=device, device_id_type=MESH,
        )

    def grad_copy(n):
        return mine(n, out_grad.at[:, pl.ds(n * HD, HD)], grads.at[n])

    own_half = pl.ds(core * (D // 2), D // 2)
    own_weights = [
        mine(LOCAL, query_weight, q_rows.at[own_half]),
        mine(LOCAL + 1, kv_weight, kv_rows.at[own_half]),
    ]
    for n in range(LOCAL):
        grad_copy(n).start()
    for copy in own_weights:
        copy.start()
    codes[core] = jnp.broadcast_to(code_row[...], (8, SL))
    gains[core] = gain[...]

    pl.semaphore_wait(barrier, len(peers))

    def from_mirror(which, n):
        source, target = ((held_query, queries), (held_output, outputs))[which]
        return remote(
            source.at[:, pl.ds(n * HD, HD)], target.at[n],
            mirror_send.at[which, n], mirror_recv.at[which, n], mirror,
        )

    own_rows = pl.ds(pl.multiple_of(core * HALF + head * OWN, 16), OWN)
    cached = ((key_cache, keys), (value_cache, values))
    for which, (source, target) in enumerate(cached):
        for i in range(1, HEADS):
            to = (head + i) % HEADS
            columns = pl.ds(pl.multiple_of(to // GROUP * HD, HD), HD)
            remote(
                source.at[:, columns], target.at[own_rows],
                gather_send.at[which], gather_recv.at[which], (section, to),
            ).start()
        columns = pl.ds(pl.multiple_of(head // GROUP * HD, HD), HD)
        pltpu.make_async_copy(
            source.at[:, columns], target.at[own_rows], gather_recv.at[which]
        ).start()

    for n in range(LOCAL):
        for which in range(2):
            from_mirror(which, n).start()

    pair_copies = [
        remote(codes.at[core], codes.at[core], pair_send.at[0], pair_recv.at[0], pair),
        remote(gains.at[core], gains.at[core], pair_send.at[1], pair_recv.at[1], pair),
        remote(query_weight, q_rows.at[own_half], pair_send.at[2], pair_recv.at[2], pair),
        remote(kv_weight, kv_rows.at[own_half], pair_send.at[3], pair_recv.at[3], pair),
    ]
    for copy in pair_copies:
        copy.start()

    pair_copies[0].wait_recv()
    here = codes[core][0:1]
    at_row = lax.broadcasted_iota(jnp.int32, (SL, SL), 0)
    at_lane = lax.broadcasted_iota(jnp.int32, (SL, SL), 1)
    code_column = jnp.sum(
        jnp.where(at_row == at_lane, here.astype(F32), 0.0), axis=1, keepdims=True
    ).astype(jnp.int32)
    both = jnp.concatenate([codes[0][0:1], codes[1][0:1]], axis=1)
    code_keys = jnp.where(core == 0, both[:, :WINDOW], both[:, 2 * SL - WINDOW :])
    token = core * SL + lax.broadcasted_iota(jnp.int32, (SL, WINDOW), 0)
    key_at = core * (2 * SL - WINDOW) + lax.broadcasted_iota(jnp.int32, (SL, WINDOW), 1)
    same_segment = (code_column >> 1) == (code_keys >> 1)
    both_image = (code_column & 1) + (code_keys & 1) == 2
    seen = same_segment & ((key_at <= token) | both_image)
    bias[...] = jnp.where(seen, 0.0, far_negative)
    kv_acc[...] = jnp.zeros_like(kv_acc)

    half_rows = pl.ds(pl.multiple_of(core * HALF, 16), HALF)
    for which, (_, target) in enumerate(cached):
        half = target.at[half_rows]
        pltpu.make_async_copy(half, half, gather_recv.at[which]).wait()
        remote(half, half, pair_send.at[4 + which], pair_recv.at[4 + which], pair).start()
    for which, (_, target) in enumerate(cached):
        half = target.at[half_rows]
        remote(half, half, pair_send.at[4 + which], pair_recv.at[4 + which], pair).wait()

    window_rows = pl.ds(pl.multiple_of(CTX + core * (2 * SL - WINDOW), 16), WINDOW)
    chunks = [(pl.ds(i, CHUNK), slice(i, i + CHUNK)) for i in range(0, CTX, CHUNK)]
    chunks.append((window_rows, slice(CTX, CTX + WINDOW)))

    def tiles(array):
        return [array[:, i : i + HD] for i in range(0, array.shape[1], HD)]

    def attention(n, carry):
        from_mirror(0, n).wait()
        query = queries[n]
        most = None
        for rows, columns in chunks:
            raw = dot_nt(query, keys[rows])
            if columns.start == CTX:
                raw = raw + bias[...]
            elif columns.stop > CTX // 2:
                at = columns.start + lax.broadcasted_iota(jnp.int32, (1, CHUNK), 1)
                raw = raw + jnp.where(at < length[0], 0.0, far_negative)
            scores[:, columns] = raw
            for tile in tiles(raw):
                most = tile if most is None else jnp.maximum(most, tile)
        most = jnp.max(most, axis=1, keepdims=True)
        total = jnp.zeros((SL, HD), F32)
        for _, columns in chunks:
            weight = jnp.exp2((scores[:, columns] - most) * factor2)
            scores[:, columns] = weight
            for tile in tiles(weight):
                total = total + tile
        total = jnp.sum(total, axis=1, keepdims=True)
        inverse = 1.0 / total
        scale = factor * inverse
        from_mirror(1, n).wait()
        grad_copy(n).wait()
        grad = grads[n]
        delta = jnp.sum(grad.astype(F32) * outputs[n].astype(F32), axis=1, keepdims=True)
        gradient = jnp.zeros((SL, HD), F32)
        for rows, columns in chunks:
            weight = scores[:, columns]
            prob_grad = dot_nt(grad, values[rows])
            score_grad = (weight * scale * (prob_grad - delta)).astype(BF16)
            gradient = gradient + jnp.dot(score_grad, keys[rows], preferred_element_type=F32)
            if columns.start == CTX:
                probs = (weight * inverse).astype(BF16)
                kv_acc[:, :HD] += dot_tn(score_grad, query)
                kv_acc[:, HD:] += dot_tn(probs, grad)
        query_grad[:, pl.ds(pl.multiple_of(n * HD, HD), HD)] = gradient.astype(BF16)
        return carry

    lax.fori_loop(0, LOCAL, attention, 0)

    other_rows = pl.ds(pl.multiple_of((1 - core) * SL, 16), WINDOW - SL)
    kv_pair = remote(kv_acc.at[other_rows], kv_other, pair_send.at[6], pair_recv.at[6], pair)
    kv_pair.start()

    for copy in own_weights:
        copy.wait()
    for copy in pair_copies[1:]:
        copy.wait_recv()

    def project(block):
        columns = slice(block * BLOCK, (block + 1) * BLOCK)
        acc[:, columns] = dot_nt(query_grad[...], q_rows[columns])

    project(0)
    kv_pair.wait_recv()
    kv_acc[WINDOW - SL : SL] += kv_other[...]
    summed = kv_acc[pl.ds(pl.multiple_of(core * (WINDOW - SL), 16), SL)]
    low = lax.broadcasted_iota(jnp.int32, (HD, HD), 1) < HD // 2
    group = head // GROUP
    place = head % GROUP
    for i in range(4):
        columns = slice(i // 2 * HD, (i // 2 + 1) * HD)
        top, bottom = summed[: SL // 2, columns], summed[SL // 2 :, columns]
        if i % 2 == 0:
            packed = jnp.where(low, top, pltpu.roll(bottom, HD // 2, 1))
        else:
            packed = jnp.where(low, pltpu.roll(top, HD // 2, 1), bottom)
        kv_out[i] = packed.astype(BF16)

    def share(i):
        to = i // 2 * (HEADS // 2) + 2 * group + i % 2
        copy = remote(
            kv_out.at[i], kv_in.at[place], share_send.at[i], share_recv.at[place], (section, to)
        )
        local = pltpu.make_async_copy(kv_out.at[i], kv_in.at[place], share_recv.at[place])
        return to, copy, local

    for i in range(4):
        to, copy, local = share(i)
        pl.when(to != head)(copy.start)
        pl.when(to == head)(local.start)
    for block in range(1, BLOCKS):
        project(block)
    for i in range(4):
        pltpu.make_async_copy(kv_out.at[i], kv_in.at[i], share_recv.at[i]).wait()
    kv_sum = kv_in[0].astype(F32) + kv_in[1].astype(F32) + kv_in[2].astype(F32) + kv_in[3].astype(F32)
    kv_part = jnp.concatenate(
        [kv_sum[:, : HD // 2], pltpu.roll(kv_sum, HD // 2, 1)[:, : HD // 2]], axis=0
    ).astype(BF16)

    def columns_of(block):
        return slice(block * BLOCK, (block + 1) * BLOCK)

    def own_part(block, at):
        if x_first(block):
            rows = pl.ds(pl.multiple_of(at * 32 + side * 16, 16), 16)
        else:
            rows = pl.ds(pl.multiple_of(at * 32, 32), 32)
        return acc[rows, columns_of(block)]

    def ring_copy(way, step, block):
        height = 16 if x_first(block) else 32
        start = block * BLOCK
        if step == 1:
            columns = pl.ds(start + way * (BLOCK // 2), BLOCK // 2)
        else:
            columns = pl.ds(start, BLOCK)
        return remote(
            ring_out.at[way, step - 1, pl.ds(0, height), columns],
            ring_in.at[way, step - 1, pl.ds(0, height), columns],
            ring_send.at[way, step - 1, block], ring_recv.at[way, step - 1, block], along[way],
        )

    def ring_step(step, block):
        height = 16 if x_first(block) else 32
        columns = columns_of(block)
        for way in range(2):
            distance = 5 - step
            at = (ring_at + (distance if way == 0 else RING - distance)) % RING
            part = own_part(block, at)
            near = slice(columns.start + way * (BLOCK // 2), columns.start + (way + 1) * (BLOCK // 2))
            if step == 1:
                half = part[:, way * (BLOCK // 2) : (way + 1) * (BLOCK // 2)]
                ring_out[way, 0, :height, near] = half.astype(BF16)
            else:
                ring_copy(way, step - 1, block).wait_recv()
                if step == 2:
                    came = ring_in[way, 0, :height, near].astype(F32)
                    halves = [part[:, : BLOCK // 2], part[:, BLOCK // 2 :]]
                    halves[way] = halves[way] + came
                    part = jnp.concatenate(halves, axis=1)
                else:
                    part = part + ring_in[way, step - 2, :height, columns].astype(F32)
                ring_out[way, step - 1, :height, columns] = part.astype(BF16)
            ring_copy(way, step, block).start()

    def x_copy(block):
        height = 128 if x_first(block) else 16
        place = pl.ds(0, height), pl.ds(block * BLOCK, BLOCK)
        return remote(x_out.at[place], x_in.at[place], x_send.at[block], x_recv.at[block], across)

    def begin(block):
        columns = columns_of(block)
        acc[:, columns] += dot_nt(kv_part, kv_rows[columns])
        if x_first(block):
            for i in range(RING):
                rows = pl.ds(pl.multiple_of(i * 32 + (1 - side) * 16, 16), 16)
                x_out[i * 16 : (i + 1) * 16, columns] = acc[rows, columns].astype(BF16)
            x_copy(block).start()
        else:
            ring_step(1, block)

    def after_x(block):
        columns = columns_of(block)
        x_copy(block).wait_recv()
        for i in range(RING):
            rows = pl.ds(pl.multiple_of(i * 32 + side * 16, 16), 16)
            acc[rows, columns] += x_in[i * 16 : (i + 1) * 16, columns].astype(F32)
        ring_step(1, block)

    def arrived(block):
        height = 16 if x_first(block) else 32
        columns = columns_of(block)
        part = own_part(block, ring_at)
        for way in range(2):
            ring_copy(way, 4, block).wait_recv()
            part = part + ring_in[way, 3, :height, columns].astype(F32)
        return part

    def end_ring(block):
        columns = columns_of(block)
        part = arrived(block)
        if x_first(block):
            normed[:, columns] = part
        else:
            normed[:, columns] = jnp.where(side == 0, part[:16], part[16:])
            x_out[:16, columns] = jnp.where(side == 0, part[16:], part[:16]).astype(BF16)
            x_copy(block).start()

    def end_x(block):
        columns = columns_of(block)
        x_copy(block).wait_recv()
        normed[:, columns] += x_in[:16, columns].astype(F32)

    def actions(block):
        ring = [lambda s=s: ring_step(s, block) for s in range(2, 5)]
        if x_first(block):
            return [lambda: begin(block), lambda: after_x(block), *ring, lambda: end_ring(block)]
        return [lambda: begin(block), *ring, lambda: end_ring(block), lambda: end_x(block)]

    plans = [actions(block) for block in range(BLOCKS)]
    for turn in range(BLOCKS + 5):
        for stage in range(6):
            if 0 <= turn - stage < BLOCKS:
                plans[turn - stage][stage]()

    values_in = layer_input[...].astype(F32)
    inverse = lax.rsqrt(jnp.sum(values_in * values_in, axis=1, keepdims=True) / D + epsilon)
    correlation = jnp.zeros((16, HD), F32)
    for t in range(D // HD):
        columns = slice(t * HD, (t + 1) * HD)
        row = gains[t // 16].astype(F32)[t % 16 : t % 16 + 1]
        weighted = row * normed[:, columns]
        normed[:, columns] = weighted
        correlation = correlation + weighted * values_in[:, columns]
    mean = jnp.sum(correlation, axis=1, keepdims=True) / D
    result[...] = (
        residual[...].astype(F32)
        + inverse * normed[...]
        - values_in * (inverse * inverse * inverse * mean)
    ).astype(BF16)

    for which, (_, target) in enumerate(cached):
        sent = target.at[pl.ds(0, (HEADS - 1) * OWN)]
        pltpu.make_async_copy(sent, sent, gather_send.at[which]).wait()
    for copy in [*pair_copies, kv_pair]:
        copy.wait_send()
    for i in range(4):
        to, copy, _ = share(i)
        pl.when(to != head)(copy.wait_send)
    for block in range(BLOCKS):
        x_copy(block).wait_send()
        for way in range(2):
            for step in range(1, 5):
                ring_copy(way, step, block).wait_send()


def body(
    out_grad,
    held_query,
    held_output,
    key_cache,
    value_cache,
    segment_ids,
    image_flags,
    cache_length,
    query_weight,
    kv_weight,
    norm_gain,
    layer_input,
    residual_grad,
):
    code_row = (segment_ids * 2 + image_flags).reshape(1, SL)
    gain = norm_gain.reshape(16, HD)
    hbm = pl.BlockSpec(memory_space=pl.ANY)
    vmem = pl.BlockSpec(memory_space=pltpu.VMEM)
    smem = pl.BlockSpec(memory_space=pltpu.SMEM)
    dma = pltpu.SemaphoreType.DMA
    return pl.pallas_call(
        kernel,
        out_shape=jax.ShapeDtypeStruct(layer_input.shape, BF16),
        in_specs=[hbm, hbm, hbm, hbm, hbm, vmem, smem, hbm, hbm, vmem, vmem, vmem],
        out_specs=vmem,
        scratch_shapes=[
            pltpu.VMEM((LOCAL, SL, HD), BF16),
            pltpu.VMEM((LOCAL, SL, HD), BF16),
            pltpu.VMEM((LOCAL, SL, HD), BF16),
            pltpu.VMEM((CTX + 2 * SL, HD), BF16),
            pltpu.VMEM((CTX + 2 * SL, HD), BF16),
            pltpu.VMEM((D, LOCAL * HD), BF16),
            pltpu.VMEM((D, HD // 2), BF16),
            pltpu.VMEM((2, 8, SL), jnp.int32),
            pltpu.VMEM((2, 16, HD), BF16),
            pltpu.VMEM((SL, CTX + WINDOW), F32),
            pltpu.VMEM((SL, WINDOW), F32),
            pltpu.VMEM((SL, LOCAL * HD), BF16),
            pltpu.VMEM((WINDOW, 2 * HD), F32),
            pltpu.VMEM((WINDOW - SL, 2 * HD), F32),
            pltpu.VMEM((4, HD, HD), BF16),
            pltpu.VMEM((4, HD, HD), BF16),
            pltpu.VMEM((SL, D), F32),
            pltpu.VMEM((128, D), BF16),
            pltpu.VMEM((128, D), BF16),
            pltpu.VMEM((2, 4, 32, D), BF16),
            pltpu.VMEM((2, 4, 32, D), BF16),
            pltpu.VMEM((16, D), F32),
            dma((LOCAL + 2,)),
            dma((2, LOCAL)),
            dma((2, LOCAL)),
            dma((2,)),
            dma((2,)),
            dma((7,)),
            dma((7,)),
            dma((4,)),
            dma((4,)),
            dma((2, 4, BLOCKS)),
            dma((2, 4, BLOCKS)),
            dma((BLOCKS,)),
            dma((BLOCKS,)),
        ],
        compiler_params=pltpu.CompilerParams(
            collective_id=0, has_side_effects=True, vmem_limit_bytes=48 * 1024 * 1024
        ),
    )(
        out_grad,
        held_query,
        held_output,
        key_cache,
        value_cache,
        code_row,
        cache_length,
        query_weight,
        kv_weight,
        gain,
        layer_input,
        residual_grad,
    )


def solution(mesh):
    both = ("section", "head")
    in_specs = (
        P(*both),
        P(*both),
        P(*both),
        P(both, None),
        P(both, None),
        P("section"),
        P("section"),
        P("section"),
        P(*both),
        P(*both),
        P("section"),
        P(both, None),
        P(both, None),
    )
    return jax.shard_map(
        body, mesh=mesh, in_specs=in_specs, out_specs=P(both, None), check_vma=False
    )
```

time: 278 us -> 105 us (0.38)
  the two profiles are of different devices: /device:TPU:1 before, /device:TPU:72 now
where the time goes in v1:
time: 105 us; the launch traced here: 104 us
  Pallas kernels  92.1 us (88%)
  local copies, waits for them, and re-layouts  10.6 us (10%)
    pallas_call x1, Pallas kernels, body(): pl.pallas_call(kernel, out_shape=jax.ShapeDtypeStruct(layer_input.shape,...  92.1 us
    unnamed x20, local copies, waits for them, and re-layouts  10.6 us

profile of v1, /device:TPU:72, one launch (start us, length us, event | category | flops | bytes accessed | tf_op | source)
XLA Modules:
  0.0 104.1 jit_solution(15724863624925392859)
XLA Ops:
  0.7 0.7 multiply_add_fusion
  1.4 1.2 %copy.14.kv_weight = bf16[2048,64]{1,0:T(8,128)(2,1)S(1)} copy(bf16[2048,64]{0,1:T(8,128)(2,1)} %param.22) | data formatting | bytes 524288 | tf_op args[9]
  2.6 0.0 copy-start
  2.6 1.6 %copy-done = bf16[2048,512]{1,0:T(8,128)(2,1)S(1)} copy-done((bf16[2048,512]{1,0:T(8,128)(2,1)S(1)}, bf16[2048,512]{1,0:T(8,128)(2,1)}, u32[]{:S(2)}) %copy-start) | copy-done | bytes 2097176
  4.2 0.0 copy-start.1
  4.2 0.9 copy-done.1
  5.1 0.0 copy-start.2
  5.1 0.9 copy-done.2
  6.1 0.0 copy-start.3
  6.1 0.9 copy-done.3
  7.0 0.0 copy-start.4
  7.0 0.9 copy-done.4
  7.9 0.0 copy-start.5
  7.9 0.9 copy-done.5
  8.8 0.0 copy-start.6
  8.8 0.9 copy-done.6
  9.7 0.0 copy-start.7
  9.7 0.9 copy-done.7
  10.6 0.0 copy-start.8
  10.6 0.7 copy-done.8
  11.3 92.1 %shard_map.127 = bf16[16,4096]{1,0:T(8,128)(2,1)S(1)} custom-call(bf16[256,512]{1,0:T(8,128)(2,1)S(1)} %copy-done.1, bf16[256,512]{1,0:T(8,128)(2,1)S(1)} %copy-done.2, bf16[256,512]{1,0:T(8,128)(2,1)S(1)} %copy-done.3, bf16[80,512]{1,0:T(8,128)(2,1)S(1)} %copy-done.6, bf16[80,512]{1,0:T(8,128)(2,1)S(1)} %copy-done.7, s32[1,256]{1,0:T(1,128)S(1)} %bitcast.3, ...), custom_call_target="tpu_custom_call" | custom-call | tf_op jit(solution)/shard_map/pallas_call | solution.py:457
  103.4 0.7 copy.17
Async XLA Ops:
  2.6 1.6 %copy-start = (bf16[2048,512]{1,0:T(8,128)(2,1)S(1)}, bf16[2048,512]{1,0:T(8,128)(2,1)}, u32[]{:S(2)}) copy-start(bf16[2048,512]{1,0:T(8,128)(2,1)} %query_weight.1) | copy-start | bytes 6291460
  4.2 0.9 copy-start.1
  5.1 0.9 copy-start.2
  6.1 0.9 copy-start.3
  7.0 0.9 copy-start.4
  7.9 0.9 copy-start.5
  8.8 0.9 copy-start.6
  9.7 0.9 copy-start.7
  10.6 0.7 copy-start.8

commit v2 on v1

--- a/solution.py
+++ b/solution.py
@@ -21,6 +21,7 @@
 GROUP = HEADS // KVH
 OWN = (CTX + 2 * SL) // 2 // HEADS
 HALF = (CTX + 2 * SL) // 2
+REACH = 64
 WINDOW = 384
 CHUNK = 512
 BLOCK = 512
@@ -32,8 +33,11 @@
 factor2 = factor / math.log(2.0)
 
 
+TURNS = tuple([0, 1, 2, 3, 4, 5, 6, 7, 1, 2, 3, 5, 6, 7, 0, 1, 2, 3, 5, 4, 6, 7, 0, 1, 2, 3, 5, 4, 6, 7, 0, 1, 2, 3, 5, 1, 4, 2, 6, 3, 7, 0, 5, 4, 6, 7, 0, 4])
+
+
 def x_first(block):
-    return block % 2 == 0
+    return block in (0, 4)
 
 
 def dot_nt(left, right):
@@ -50,7 +54,8 @@
     held_output,
     key_cache,
     value_cache,
-    code_row,
+    segments,
+    flags,
     length,
     query_weight,
     kv_weight,
@@ -71,9 +76,14 @@
     bias,
     query_grad,
     kv_acc,
-    kv_other,
     kv_out,
     kv_in,
+    reach_out,
+    reach_in,
+    segments_here,
+    flags_here,
+    input_here,
+    residual_here,
     acc,
     x_out,
     x_in,
@@ -87,6 +97,8 @@
     gather_recv,
     pair_send,
     pair_recv,
+    home_send,
+    home_recv,
     share_send,
     share_recv,
     ring_send,
@@ -105,7 +117,9 @@
     along = ((section, (head + 2) % HEADS), (section, (head + HEADS - 2) % HEADS))
 
     barrier = pltpu.get_barrier_semaphore()
-    peers = [mirror, pair] + [(section, (head + i) % HEADS) for i in range(1, HEADS)]
+    group_start = head // GROUP * GROUP
+    peers = [mirror] + [(section, (head + i) % HEADS) for i in range(1, HEADS)]
+    peers += [(pair[0], group_start + (head + i) % GROUP) for i in range(GROUP)]
     for peer in peers:
         pl.semaphore_signal(barrier, inc=1, device_id=peer, device_id_type=MESH)
 
@@ -121,18 +135,20 @@
     def grad_copy(n):
         return mine(n, out_grad.at[:, pl.ds(n * HD, HD)], grads.at[n])
 
-    own_half = pl.ds(core * (D // 2), D // 2)
-    own_weights = [
-        mine(LOCAL, query_weight, q_rows.at[own_half]),
-        mine(LOCAL + 1, kv_weight, kv_rows.at[own_half]),
-    ]
+    own_half = pl.ds(pl.multiple_of(core * (D // 2), D // 2), D // 2)
+    own_weight = mine(LOCAL, query_weight, q_rows.at[own_half])
     for n in range(LOCAL):
         grad_copy(n).start()
-    for copy in own_weights:
+    own_weight.start()
+    small = [
+        mine(LOCAL + 1, segments, segments_here),
+        mine(LOCAL + 2, flags, flags_here),
+        mine(LOCAL + 3, gain, gains.at[core]),
+        mine(LOCAL + 4, layer_input, input_here),
+        mine(LOCAL + 5, residual, residual_here),
+    ]
+    for copy in small:
         copy.start()
-    codes[core] = jnp.broadcast_to(code_row[...], (8, SL))
-    gains[core] = gain[...]
-
     pl.semaphore_wait(barrier, len(peers))
 
     def from_mirror(which, n):
@@ -161,11 +177,24 @@
         for which in range(2):
             from_mirror(which, n).start()
 
+    quarter = head // (HEADS // 2) * 2 + head % 2
+    kv_home = head % (HEADS // 2) // 2 * GROUP + quarter
+    kv_half = kv_rows.at[:, own_half]
+    kv_away = remote(kv_weight, kv_half, home_send, home_recv, (section, kv_home))
+    kv_here = pltpu.make_async_copy(kv_weight, kv_half, home_recv)
+    kv_arrival = pltpu.make_async_copy(kv_half, kv_half, home_recv)
+    kv_forward = remote(kv_half, kv_half, pair_send.at[3], pair_recv.at[3], pair)
+    pl.when(kv_home != head)(kv_away.start)
+    pl.when(kv_home == head)(kv_here.start)
+
+    small[0].wait()
+    small[1].wait()
+    codes[core] = jnp.broadcast_to(segments_here[...] * 2 + flags_here[...], (8, SL))
+    small[2].wait()
     pair_copies = [
         remote(codes.at[core], codes.at[core], pair_send.at[0], pair_recv.at[0], pair),
         remote(gains.at[core], gains.at[core], pair_send.at[1], pair_recv.at[1], pair),
         remote(query_weight, q_rows.at[own_half], pair_send.at[2], pair_recv.at[2], pair),
-        remote(kv_weight, kv_rows.at[own_half], pair_send.at[3], pair_recv.at[3], pair),
     ]
     for copy in pair_copies:
         copy.start()
@@ -246,12 +275,9 @@
 
     lax.fori_loop(0, LOCAL, attention, 0)
 
-    other_rows = pl.ds(pl.multiple_of((1 - core) * SL, 16), WINDOW - SL)
-    kv_pair = remote(kv_acc.at[other_rows], kv_other, pair_send.at[6], pair_recv.at[6], pair)
-    kv_pair.start()
-
-    for copy in own_weights:
-        copy.wait()
+    kv_arrival.wait()
+    kv_forward.start()
+    own_weight.wait()
     for copy in pair_copies[1:]:
         copy.wait_recv()
 
@@ -259,42 +285,59 @@
         columns = slice(block * BLOCK, (block + 1) * BLOCK)
         acc[:, columns] = dot_nt(query_grad[...], q_rows[columns])
 
-    project(0)
-    kv_pair.wait_recv()
-    kv_acc[WINDOW - SL : SL] += kv_other[...]
-    summed = kv_acc[pl.ds(pl.multiple_of(core * (WINDOW - SL), 16), SL)]
-    low = lax.broadcasted_iota(jnp.int32, (HD, HD), 1) < HD // 2
+    own_keys = kv_acc[pl.ds(pl.multiple_of(core * (WINDOW - SL), 16), SL)]
+    other_keys = kv_acc[pl.ds(pl.multiple_of(SL - core * (SL - REACH), 16), REACH)]
     group = head // GROUP
     place = head % GROUP
-    for i in range(4):
+
+    def both_lanes(array, upper):
+        turned = pltpu.roll(array, HD // 2, 1)
+        low = lax.broadcasted_iota(jnp.int32, array.shape, 1) < HD // 2
+        return jnp.where(low, turned, array) if upper else jnp.where(low, array, turned)
+
+    low = lax.broadcasted_iota(jnp.int32, (HD, HD), 1) < HD // 2
+    for i in range(GROUP):
         columns = slice(i // 2 * HD, (i // 2 + 1) * HD)
-        top, bottom = summed[: SL // 2, columns], summed[SL // 2 :, columns]
-        if i % 2 == 0:
-            packed = jnp.where(low, top, pltpu.roll(bottom, HD // 2, 1))
-        else:
-            packed = jnp.where(low, pltpu.roll(top, HD // 2, 1), bottom)
-        kv_out[i] = packed.astype(BF16)
+        top = both_lanes(own_keys[: SL // 2, columns], i % 2)
+        bottom = both_lanes(own_keys[SL // 2 :, columns], i % 2)
+        kv_out[i] = jnp.where(low, top, bottom).astype(BF16)
+        reach_out[i] = both_lanes(other_keys[:, columns], i % 2).astype(BF16)
 
     def share(i):
-        to = i // 2 * (HEADS // 2) + 2 * group + i % 2
+        to = group * GROUP + i
         copy = remote(
-            kv_out.at[i], kv_in.at[place], share_send.at[i], share_recv.at[place], (section, to)
+            kv_out.at[i], kv_in.at[place], share_send.at[0, i], share_recv.at[0, place],
+            (section, to),
         )
-        local = pltpu.make_async_copy(kv_out.at[i], kv_in.at[place], share_recv.at[place])
-        return to, copy, local
-
-    for i in range(4):
-        to, copy, local = share(i)
-        pl.when(to != head)(copy.start)
-        pl.when(to == head)(local.start)
-    for block in range(1, BLOCKS):
+        local = pltpu.make_async_copy(kv_out.at[i], kv_in.at[place], share_recv.at[0, place])
+        reach = remote(
+            reach_out.at[i], reach_in.at[place], share_send.at[1, i], share_recv.at[1, place],
+            (pair[0], to),
+        )
+        return copy, local, reach
+
+    for i in range(GROUP):
+        copy, local, reach = share(i)
+        pl.when(i != place)(copy.start)
+        pl.when(i == place)(local.start)
+        reach.start()
+    for block in range(BLOCKS):
         project(block)
-    for i in range(4):
-        pltpu.make_async_copy(kv_out.at[i], kv_in.at[i], share_recv.at[i]).wait()
-    kv_sum = kv_in[0].astype(F32) + kv_in[1].astype(F32) + kv_in[2].astype(F32) + kv_in[3].astype(F32)
+    kv_sum = jnp.zeros((HD, HD), F32)
+    reach_sum = jnp.zeros((REACH, HD), F32)
+    for i in range(GROUP):
+        pltpu.make_async_copy(kv_out.at[i], kv_in.at[i], share_recv.at[0, i]).wait()
+        kv_sum = kv_sum + kv_in[i].astype(F32)
+        pltpu.make_async_copy(reach_out.at[i], reach_in.at[i], share_recv.at[1, i]).wait()
+        reach_sum = reach_sum + reach_in[i].astype(F32)
+    lane_half = lax.broadcasted_iota(jnp.int32, (REACH, HD), 1) // (HD // 2)
+    reach_sum = jnp.where(lane_half == 1 - core, reach_sum, 0.0)
+    second = core.astype(F32)
+    kv_sum = kv_sum + jnp.concatenate([reach_sum * second, reach_sum * (1.0 - second)], axis=0)
     kv_part = jnp.concatenate(
         [kv_sum[:, : HD // 2], pltpu.roll(kv_sum, HD // 2, 1)[:, : HD // 2]], axis=0
     ).astype(BF16)
+    kv_forward.wait_recv()
 
     def columns_of(block):
         return slice(block * BLOCK, (block + 1) * BLOCK)
@@ -349,7 +392,7 @@
 
     def begin(block):
         columns = columns_of(block)
-        acc[:, columns] += dot_nt(kv_part, kv_rows[columns])
+        acc[:, columns] += jnp.dot(kv_part, kv_rows[:, columns], preferred_element_type=F32)
         if x_first(block):
             for i in range(RING):
                 rows = pl.ds(pl.multiple_of(i * 32 + (1 - side) * 16, 16), 16)
@@ -397,12 +440,12 @@
         return [lambda: begin(block), *ring, lambda: end_ring(block), lambda: end_x(block)]
 
     plans = [actions(block) for block in range(BLOCKS)]
-    for turn in range(BLOCKS + 5):
-        for stage in range(6):
-            if 0 <= turn - stage < BLOCKS:
-                plans[turn - stage][stage]()
-
-    values_in = layer_input[...].astype(F32)
+    for block in TURNS:
+        plans[block].pop(0)()
+
+    small[3].wait()
+    small[4].wait()
+    values_in = input_here[...].astype(F32)
     inverse = lax.rsqrt(jnp.sum(values_in * values_in, axis=1, keepdims=True) / D + epsilon)
     correlation = jnp.zeros((16, HD), F32)
     for t in range(D // HD):
@@ -413,7 +456,7 @@
         correlation = correlation + weighted * values_in[:, columns]
     mean = jnp.sum(correlation, axis=1, keepdims=True) / D
     result[...] = (
-        residual[...].astype(F32)
+        residual_here[...].astype(F32)
         + inverse * normed[...]
         - values_in * (inverse * inverse * inverse * mean)
     ).astype(BF16)
@@ -421,11 +464,13 @@
     for which, (_, target) in enumerate(cached):
         sent = target.at[pl.ds(0, (HEADS - 1) * OWN)]
         pltpu.make_async_copy(sent, sent, gather_send.at[which]).wait()
-    for copy in [*pair_copies, kv_pair]:
+    for copy in [*pair_copies, kv_forward]:
         copy.wait_send()
-    for i in range(4):
-        to, copy, _ = share(i)
-        pl.when(to != head)(copy.wait_send)
+    pl.when(kv_home != head)(kv_away.wait_send)
+    for i in range(GROUP):
+        copy, _, reach = share(i)
+        pl.when(i != place)(copy.wait_send)
+        reach.wait_send()
     for block in range(BLOCKS):
         x_copy(block).wait_send()
         for way in range(2):
@@ -448,16 +493,15 @@
     layer_input,
     residual_grad,
 ):
-    code_row = (segment_ids * 2 + image_flags).reshape(1, SL)
     gain = norm_gain.reshape(16, HD)
-    hbm = pl.BlockSpec(memory_space=pl.ANY)
+    hbm = pl.BlockSpec(memory_space=pltpu.HBM)
     vmem = pl.BlockSpec(memory_space=pltpu.VMEM)
     smem = pl.BlockSpec(memory_space=pltpu.SMEM)
     dma = pltpu.SemaphoreType.DMA
     return pl.pallas_call(
         kernel,
         out_shape=jax.ShapeDtypeStruct(layer_input.shape, BF16),
-        in_specs=[hbm, hbm, hbm, hbm, hbm, vmem, smem, hbm, hbm, vmem, vmem, vmem],
+        in_specs=[hbm] * 7 + [smem] + [hbm] * 5,
         out_specs=vmem,
         scratch_shapes=[
             pltpu.VMEM((LOCAL, SL, HD), BF16),
@@ -466,38 +510,45 @@
             pltpu.VMEM((CTX + 2 * SL, HD), BF16),
             pltpu.VMEM((CTX + 2 * SL, HD), BF16),
             pltpu.VMEM((D, LOCAL * HD), BF16),
-            pltpu.VMEM((D, HD // 2), BF16),
+            pltpu.VMEM((HD // 2, D), BF16),
             pltpu.VMEM((2, 8, SL), jnp.int32),
             pltpu.VMEM((2, 16, HD), BF16),
             pltpu.VMEM((SL, CTX + WINDOW), F32),
             pltpu.VMEM((SL, WINDOW), F32),
             pltpu.VMEM((SL, LOCAL * HD), BF16),
             pltpu.VMEM((WINDOW, 2 * HD), F32),
-            pltpu.VMEM((WINDOW - SL, 2 * HD), F32),
-            pltpu.VMEM((4, HD, HD), BF16),
-            pltpu.VMEM((4, HD, HD), BF16),
+            pltpu.VMEM((GROUP, HD, HD), BF16),
+            pltpu.VMEM((GROUP, HD, HD), BF16),
+            pltpu.VMEM((GROUP, REACH, HD), BF16),
+            pltpu.VMEM((GROUP, REACH, HD), BF16),
+            pltpu.VMEM((1, SL), jnp.int32),
+            pltpu.VMEM((1, SL), jnp.int32),
+            pltpu.VMEM((16, D), BF16),
+            pltpu.VMEM((16, D), BF16),
             pltpu.VMEM((SL, D), F32),
             pltpu.VMEM((128, D), BF16),
             pltpu.VMEM((128, D), BF16),
             pltpu.VMEM((2, 4, 32, D), BF16),
             pltpu.VMEM((2, 4, 32, D), BF16),
             pltpu.VMEM((16, D), F32),
-            dma((LOCAL + 2,)),
+            dma((LOCAL + 6,)),
             dma((2, LOCAL)),
             dma((2, LOCAL)),
             dma((2,)),
             dma((2,)),
-            dma((7,)),
-            dma((7,)),
-            dma((4,)),
-            dma((4,)),
+            dma((6,)),
+            dma((6,)),
+            dma,
+            dma,
+            dma((2, GROUP)),
+            dma((2, GROUP)),
             dma((2, 4, BLOCKS)),
             dma((2, 4, BLOCKS)),
             dma((BLOCKS,)),
             dma((BLOCKS,)),
         ],
         compiler_params=pltpu.CompilerParams(
-            collective_id=0, has_side_effects=True, vmem_limit_bytes=48 * 1024 * 1024
+            collective_id=0, has_side_effects=True, vmem_limit_bytes=60 * 1024 * 1024
         ),
     )(
         out_grad,
@@ -505,10 +556,11 @@
         held_output,
         key_cache,
         value_cache,
-        code_row,
+        segment_ids.reshape(1, SL),
+        image_flags.reshape(1, SL),
         cache_length,
         query_weight,
-        kv_weight,
+        kv_weight.T,
         gain,
         layer_input,
         residual_grad,

time: 105 us -> 83.4 us (0.79)
  the two profiles are of different devices: /device:TPU:72 before, /device:TPU:8 now
where the time goes in v2:
time: 83.4 us; the launch traced here: 83.2 us
  Pallas kernels  81 us (97%)
  local copies, waits for them, and re-layouts  1.57 us (2%)
    pallas_call x1, Pallas kernels, body(): pl.pallas_call(kernel, out_shape=jax.ShapeDtypeStruct(layer_input.shape,...  81 us

profile of v2, /device:TPU:8, one launch (start us, length us, event | category | flops | bytes accessed | tf_op | source)
XLA Modules:
  0.0 83.2 jit_solution(16301118511060409697)
XLA Ops:
  0.7 81.0 %shard_map.127 = bf16[16,4096]{1,0:T(8,128)(2,1)} custom-call(bf16[256,512]{1,0:T(8,128)(2,1)} %out_grad.1, bf16[256,512]{1,0:T(8,128)(2,1)} %held_query.1, bf16[256,512]{1,0:T(8,128)(2,1)} %held_output.1, bf16[80,512]{1,0:T(8,128)(2,1)} %key_cache.1, bf16[80,512]{1,0:T(8,128)(2,1)} %value_cache.1, s32[1,256]{1,0:T(1,128)} %bitcast.6, s32[1,256]{1,0:T(1,128)} %bitcast.7, ...), custom_call_target="tpu_custom_call" | custom-call | tf_op jit(solution)/shard_map/pallas_call | solution.py:501
  81.7 1.6 %copy.16 = bf16[16,4096]{1,0:T(8,128)(2,1)} copy(bf16[16,4096]{1,0:T(8,128)(2,1)} %shard_map.127) | data formatting | bytes 262144

commit v3 on v2

--- a/solution.py
+++ b/solution.py
@@ -33,11 +33,11 @@
 factor2 = factor / math.log(2.0)
 
 
-TURNS = tuple([0, 1, 2, 3, 4, 5, 6, 7, 1, 2, 3, 5, 6, 7, 0, 1, 2, 3, 5, 4, 6, 7, 0, 1, 2, 3, 5, 4, 6, 7, 0, 1, 2, 3, 5, 1, 4, 2, 6, 3, 7, 0, 5, 4, 6, 7, 0, 4])
+TURNS = (0, 1, 2, 3, 4, 5, 6, 7, 1, 2, 3, 4, 5, 7, 0, 1, 2, 3, 6, 4, 5, 7, 0, 1, 2, 3, 6, 4, 5, 7, 0, 1, 2, 3, 6, 4, 1, 5, 2, 7, 3, 0, 6, 4, 5, 7, 0, 6)
 
 
 def x_first(block):
-    return block in (0, 4)
+    return block in (0, 6)
 
 
 def dot_nt(left, right):
@@ -158,6 +158,10 @@
             mirror_send.at[which, n], mirror_recv.at[which, n], mirror,
         )
 
+    for n in range(LOCAL):
+        for which in range(2):
+            from_mirror(which, n).start()
+
     own_rows = pl.ds(pl.multiple_of(core * HALF + head * OWN, 16), OWN)
     cached = ((key_cache, keys), (value_cache, values))
     for which, (source, target) in enumerate(cached):
@@ -173,9 +177,6 @@
             source.at[:, columns], target.at[own_rows], gather_recv.at[which]
         ).start()
 
-    for n in range(LOCAL):
-        for which in range(2):
-            from_mirror(which, n).start()
 
     quarter = head // (HEADS // 2) * 2 + head % 2
     kv_home = head % (HEADS // 2) // 2 * GROUP + quarter
@@ -184,8 +185,6 @@
     kv_here = pltpu.make_async_copy(kv_weight, kv_half, home_recv)
     kv_arrival = pltpu.make_async_copy(kv_half, kv_half, home_recv)
     kv_forward = remote(kv_half, kv_half, pair_send.at[3], pair_recv.at[3], pair)
-    pl.when(kv_home != head)(kv_away.start)
-    pl.when(kv_home == head)(kv_here.start)
 
     small[0].wait()
     small[1].wait()
@@ -221,6 +220,8 @@
         half = target.at[half_rows]
         pltpu.make_async_copy(half, half, gather_recv.at[which]).wait()
         remote(half, half, pair_send.at[4 + which], pair_recv.at[4 + which], pair).start()
+    pl.when(kv_home != head)(kv_away.start)
+    pl.when(kv_home == head)(kv_here.start)
     for which, (_, target) in enumerate(cached):
         half = target.at[half_rows]
         remote(half, half, pair_send.at[4 + which], pair_recv.at[4 + which], pair).wait()

time: 83.4 us -> 80.8 us (0.969)
  the two profiles are of different devices: /device:TPU:8 before, /device:TPU:64 now
where the time goes in v3:
time: 80.8 us; the launch traced here: 80.6 us
  Pallas kernels  78.4 us (97%)
  local copies, waits for them, and re-layouts  1.57 us (2%)
    pallas_call x1, Pallas kernels, body(): pl.pallas_call(kernel, out_shape=jax.ShapeDtypeStruct(layer_input.shape,...  78.4 us

profile of v3, /device:TPU:64, one launch (start us, length us, event | category | flops | bytes accessed | tf_op | source)
XLA Modules:
  0.0 80.6 jit_solution(15148014121464689017)
XLA Ops:
  0.7 78.4 %shard_map.127 = bf16[16,4096]{1,0:T(8,128)(2,1)} custom-call(bf16[256,512]{1,0:T(8,128)(2,1)} %out_grad.1, bf16[256,512]{1,0:T(8,128)(2,1)} %held_query.1, bf16[256,512]{1,0:T(8,128)(2,1)} %held_output.1, bf16[80,512]{1,0:T(8,128)(2,1)} %key_cache.1, bf16[80,512]{1,0:T(8,128)(2,1)} %value_cache.1, s32[1,256]{1,0:T(1,128)} %bitcast.6, s32[1,256]{1,0:T(1,128)} %bitcast.7, ...), custom_call_target="tpu_custom_call" | custom-call | tf_op jit(solution)/shard_map/pallas_call | solution.py:502
  79.1 1.6 %copy.16 = bf16[16,4096]{1,0:T(8,128)(2,1)} copy(bf16[16,4096]{1,0:T(8,128)(2,1)} %shard_map.127) | data formatting | bytes 262144
